TPU v7x, 32 devices: a whole 2x2x4 slice. The times are simulated.
32 devices in a mesh: src: 8 (over y, x, core), dst: 4 (over z).
Axes of the slice: x: 2, y: 2, z: 4, core: 2. Of those that a mesh axis runs over, the one named last changes fastest.
Arguments:
- src_table: float32 [512, 8, 400], P('dst', 'src'), may hold values from -1.8 to 1.8
- src_state: float32 [512, 8], P('dst', 'src'), may hold values from 0.05 to 2
- dst_table: float32 [1024, 4, 400], P('src', 'dst'), may hold values from -20 to 20
- dst_state: float32 [1024, 4], P('src', 'dst'), may hold values from 0.05 to 2
- rel_table: float32 [16, 400], replicated, may hold values from 0.1 to 1.9
- rel_state: float32 [16], replicated, may hold values from 0.5 to 5
- src_rows: int32 [8, 4, 4096], P('src', 'dst'), may hold values from 0 to 511
- dst_rows: int32 [8, 4, 4096], P('src', 'dst'), may hold values from 0 to 1023
- rel_ids: int32 [8, 4, 4096], P('src', 'dst'), may hold values from 0 to 15
- counts: int32 [8, 4], P('src', 'dst'), may hold values from 256 to 4096, as said below
- neg_rows: int32 [8, 4, 4, 1024], P('src', 'dst'), may hold values from 0 to 1023
Outputs:
- new_src: float32 [512, 8, 400], P('dst', 'src')
- new_src_state: float32 [512, 8], P('dst', 'src')
- new_dst: float32 [1024, 4, 400], P('src', 'dst')
- new_dst_state: float32 [1024, 4], P('src', 'dst')
- new_rel: float32 [16, 400], replicated
- new_rel_state: float32 [16], replicated
Inputs may be any that keep to these rules, and one draw needn't show every extreme that they name: One bucket holds at most 4096 edges; only the first counts[i, j] slots of a bucket are real edges.
All inputs are finite; a program needn't handle non-finite values.
Results may differ from a plain program's by a relative error of at most 0.0093.
Values may be sent and summed in bfloat16 or wider, within the bound.
A program may use at most 128 MiB of HBM per device.

v0:
```python
import jax
import jax.numpy as jnp
from jax import lax
from jax.sharding import PartitionSpec as P

LEARN_RATE = 0.1


def block_terms(
    start, width_block, block_index, src_part, dst_part, rel_table, s_all, t_all, r_all, negs, count
):
    src_idx = lax.dynamic_slice_in_dim(s_all, start, width_block)
    dst_idx = lax.dynamic_slice_in_dim(t_all, start, width_block)
    rel_idx = lax.dynamic_slice_in_dim(r_all, start, width_block)
    neg_idx = lax.dynamic_index_in_dim(negs, block_index, 0, keepdims=False)
    slots = start + jnp.arange(width_block, dtype=jnp.int32)
    valid = (slots < count).astype(jnp.float32)
    onehot = (rel_idx[:, None] == jnp.arange(rel_table.shape[0], dtype=jnp.int32)[None, :]).astype(
        jnp.float32
    )
    rel_rows = jnp.dot(onehot, rel_table, precision=lax.Precision.HIGHEST)
    src_emb = jnp.take(src_part, src_idx, axis=0)
    src_wide = src_emb.astype(jnp.float32)
    query = (src_wide * rel_rows).astype(jnp.bfloat16)
    query_wide = query.astype(jnp.float32)
    dst_emb = jnp.take(dst_part, dst_idx, axis=0)
    dst_wide = dst_emb.astype(jnp.float32)
    neg_emb = jnp.take(dst_part, neg_idx, axis=0)
    pos = jnp.sum(query_wide * dst_wide, axis=-1)
    neg = lax.dot_general(
        query, neg_emb, (((1,), (1,)), ((), ())), preferred_element_type=jnp.float32
    )
    top = jnp.maximum(pos, jnp.max(neg, axis=-1))
    pos_exp = jnp.exp(pos - top)
    neg_exp = jnp.exp(neg - top[:, None])
    total = pos_exp + jnp.sum(neg_exp, axis=-1)
    pos_coef = valid * (pos_exp / total - 1.0)
    neg_weight = (valid[:, None] * neg_exp / total[:, None]).astype(jnp.bfloat16)
    dquery = (
        jnp.dot(neg_weight, neg_emb, preferred_element_type=jnp.float32)
        + pos_coef[:, None] * dst_wide
    )
    src_term = dquery * rel_rows
    rel_term = lax.dot_general(
        onehot, dquery * src_wide, (((0,), (0,)), ((), ())), precision=lax.Precision.HIGHEST
    )
    dst_pos = pos_coef[:, None] * query_wide
    dst_neg = lax.dot_general(
        neg_weight, query, (((0,), (0,)), ((), ())), preferred_element_type=jnp.float32
    )
    return (src_idx, src_term, dst_idx, dst_pos, neg_idx, dst_neg, rel_term)


def adagrad(table, state, grad):
    new_state = state + jnp.mean(grad * grad, axis=-1)
    return (table - LEARN_RATE * grad / jnp.sqrt(new_state)[..., None], new_state)


def body(
    src_table,
    src_state,
    dst_table,
    dst_state,
    rel_table,
    rel_state,
    src_rows,
    dst_rows,
    rel_ids,
    counts,
    neg_rows,
):
    rows, _, width = src_table.shape
    src_part = lax.all_gather(src_table.astype(jnp.bfloat16), "dst", axis=0, tiled=True).reshape(
        -1, width
    )
    dst_part = lax.all_gather(dst_table.astype(jnp.bfloat16), "src", axis=0, tiled=True).reshape(
        -1, width
    )
    s_all = src_rows.reshape(-1)
    t_all = dst_rows.reshape(-1)
    r_all = rel_ids.reshape(-1)
    negs = neg_rows.reshape(neg_rows.shape[2], neg_rows.shape[3])
    count = counts.reshape(())
    blocks = negs.shape[0]
    width_block = s_all.shape[0] // blocks
    active = (count + width_block - 1) // width_block

    def accumulate(block_index, carry):
        src_grad, dst_grad, rel_grad = carry
        start = block_index * width_block
        src_idx, src_term, dst_idx, dst_pos, neg_idx, dst_neg, rel_term = block_terms(
            start,
            width_block,
            block_index,
            src_part,
            dst_part,
            rel_table,
            s_all,
            t_all,
            r_all,
            negs,
            count,
        )
        src_grad = src_grad.at[src_idx].add(src_term)
        dst_grad = dst_grad.at[dst_idx].add(dst_pos).at[neg_idx].add(dst_neg)
        return (src_grad, dst_grad, rel_grad + rel_term)

    start = (
        jnp.zeros(src_part.shape, jnp.float32),
        jnp.zeros(dst_part.shape, jnp.float32),
        jnp.zeros(rel_table.shape, jnp.float32),
    )
    src_sum, dst_sum, rel_sum = lax.fori_loop(0, active, accumulate, start)
    src_grad = lax.psum_scatter(src_sum, "dst", scatter_dimension=0, tiled=True)
    dst_grad = lax.psum_scatter(dst_sum, "src", scatter_dimension=0, tiled=True)
    rel_grad = lax.psum(rel_sum, ("src", "dst"))
    new_src, new_src_state = adagrad(src_table, src_state, src_grad.reshape(src_table.shape))
    new_dst, new_dst_state = adagrad(dst_table, dst_state, dst_grad.reshape(dst_table.shape))
    new_rel, new_rel_state = adagrad(rel_table, rel_state, rel_grad)
    return (new_src, new_src_state, new_dst, new_dst_state, new_rel, new_rel_state)


def solution(mesh):
    return jax.shard_map(
        body,
        mesh=mesh,
        in_specs=(
            P("dst", "src", None),
            P("dst", "src"),
            P("src", "dst", None),
            P("src", "dst"),
            P(),
            P(),
            P("src", "dst", None),
            P("src", "dst", None),
            P("src", "dst", None),
            P("src", "dst"),
            P("src", "dst", None, None),
        ),
        out_specs=(
            P("dst", "src", None),
            P("dst", "src"),
            P("src", "dst", None),
            P("src", "dst"),
            P(),
            P(),
        ),
        check_vma=False,
    )
```

profile of v0, /device:TPU:1, one launch (start us, length us, event | category | flops | bytes accessed | tf_op | source)
XLA Modules:
  0.0 402.0 jit_solution(13824094178717480334)
XLA Ops:
  7.9 0.9 convert_element_type.47
  8.8 0.9 convert_element_type.48
  9.8 13.5 %all_gather.6 = bf16[512,1,400]{0,2,1:T(8,128)(2,1)S(1)} all-gather(bf16[128,1,400]{0,2,1:T(8,128)(2,1)S(1)} %convert_element_type.47), channel_id=1, replica_groups=mesh['src'=8,'dst'=4] {'dst'}, dimensions={0}, use_global_device_ids=true | all-gather | bytes 512000 | tf_op jit(solution)/shard_map/all_gather | solution.py:73
  23.3 1.0 copy.37
  24.3 12.5 %all_gather.7 = bf16[1024,1,400]{0,2,1:T(8,128)(2,1)S(1)} all-gather(bf16[128,1,400]{0,2,1:T(8,128)(2,1)S(1)} %convert_element_type.48), channel_id=1, replica_groups=mesh['src'=8,'dst'=4] {'src'}, dimensions={0}, use_global_device_ids=true | all-gather | bytes 921600 | tf_op jit(solution)/shard_map/all_gather | solution.py:76
  36.8 1.3 copy.38
  38.5 71.8 %while.16 = (s32[]{:T(128)}, f32[512,400]{1,0:T(8,128)S(1)}, f32[1024,400]{1,0:T(8,128)S(1)}, f32[16,400]{1,0:T(8,128)S(1)}, s32[]{:T(128)}, /*index=5*/s32[4096...) while((s32[]{:T(128)}, f32[512,400]{1,0:T(8,128)S(1)}, ...), condition=%wide.region_7.9_spmd, body=%wide.region_0.8_spmd.sunk | while | flops 2691130624 | bytes 81392016 | solution.py:113
  40.6 1.3 compare_and_fusion.7
  42.0 6.5 %gather_fusion.2 = bf16[1024,400]{1,0:T(8,128)(2,1)} fusion(bf16[1024,400]{1,0:T(8,128)(2,1)} %get-tuple-element.396, s32[1024]{0:T(1024)S(1)} %fusion.49), kind=kCustom, calls=%fused_computation.clone.clone.1 | custom fusion | bytes 1642496 | tf_op jit(solution)/shard_map/while/body/jit(_take)/gather | solution.py:28
  48.5 6.5 %gather_fusion = bf16[1024,400]{1,0:T(8,128)(2,1)} fusion(bf16[1024,400]{1,0:T(8,128)(2,1)} %get-tuple-element.396, s32[1024]{0:T(1024)S(1)} %broadcast_clamp_fusion.4), kind=kCustom, calls=%fused_computation.1.clone.clone.1 | custom fusion | bytes 1642496 | tf_op jit(solution)/shard_map/while/body/jit(_take)/gather | solution.py:26
  54.9 2.2 copy.46
  57.2 6.2 %gather_fusion.1 = bf16[1024,400]{1,0:T(8,128)(2,1)} fusion(bf16[512,400]{1,0:T(8,128)(2,1)} %get-tuple-element.392, s32[1024]{0:T(1024)S(1)} %broadcast_clamp_fusion.5), kind=kCustom, calls=%fused_computation.2.clone.1 | custom fusion | bytes 1642496 | tf_op jit(solution)/shard_map/while/body/jit(_take)/gather | solution.py:22
  63.4 2.2 copy.47
  65.5 2.8 fusion.48
  68.4 1.3 fusion.50
  72.1 2.4 fusion.52
  74.5 2.6 fusion.53
  77.1 1.2 fusion.54
  78.3 2.8 copy.48
  81.2 7.7 %scatter_fusion = f32[512,400]{1,0:T(8,128)S(1)} fusion(f32[512,400]{1,0:T(8,128)S(1)} %get-tuple-element.368, s32[1024]{0:T(1024)S(1)} %get-tuple-element.333, f32[1024,400]{1,0:T(8,128)} %copy.48), kind=kCustom, calls=%fused_computation.3.clone.1 | custom fusion | flops 409600 | bytes 4919296 | tf_op jit(solution)/shard_map/while/body/scatter-add | solution.py:104
  88.8 2.6 convert_multiply_fusion.11
  91.4 2.8 copy.49
  94.2 8.0 %scatter_fusion.1 = f32[1024,400]{1,0:T(8,128)S(1)} fusion(f32[1024,400]{1,0:T(8,128)S(1)} %get-tuple-element.369, s32[1024]{0:T(1024)S(1)} %get-tuple-element.334, f32[1024,400]{1,0:T(8,128)} %copy.49), kind=kCustom, calls=%fused_computation.4.clone.1 | custom fusion | flops 409600 | bytes 4919296 | tf_op jit(solution)/shard_map/while/body/scatter-add | solution.py:105
  102.3 8.0 %scatter_fusion.2 = f32[1024,400]{1,0:T(8,128)S(1)} fusion(f32[1024,400]{1,0:T(8,128)S(1)} %scatter_fusion.1, s32[1024]{0:T(1024)S(1)} %bitcast.51, f32[1024,400]{1,0:T(8,128)} %fusion.53), kind=kCustom, calls=%fused_computation.5.clone.1 | custom fusion | flops 409600 | bytes 4919296 | tf_op jit(solution)/shard_map/while/body/scatter-add | solution.py:105
  110.3 1.2 copy.39
  111.6 1.7 copy.40
  113.4 252.7 %psum.7 = f32[16,400]{1,0:T(8,128)S(1)} all-reduce(f32[16,400]{1,0:T(8,128)S(1)} %get-tuple-element.175), channel_id=1, replica_groups=mesh['src'=8,'dst'=4] {'src','dst'}, use_global_device_ids=true, to_apply=%region_12.14 | all-reduce | flops 6400 | bytes 51200 | tf_op jit(solution)/shard_map/psum | solution.py:116
  367.4 1.0 multiply_reduce_fusion.1
  368.9 1.6 bitcast_subtract_fusion.1
  370.6 21.4 %reduce-scatter.5.cloned.1.call-done = f32[128,400]{0,1:T(8,128)} async-done(((f32[1024,400]{0,1:T(8,128)}), f32[128,400]{0,1:T(8,128)}) %reduce-scatter.5.cloned.1.call-update) | async-done | bytes 204816 | tf_op jit(solution)/shard_map/reduce_scatter | solution.py:115
  392.0 1.0 multiply_reduce_fusion
  393.5 1.6 bitcast_subtract_fusion
  (44 shorter events, 7.4 us)
Async XLA Ops:
  7.2 360.3 %reduce-scatter.3.cloned.1.call-start = ((), (), s32[]{:S(2)}) async-start(), calls=%async_computation.2 | async-start | bytes 1024000 | tf_op jit(solution)/shard_map/reduce_scatter | solution.py:114
  36.8 1.7 copy-start.4
  65.5 2.8 copy-start.2
  68.3 6.2 %copy-start.3 = (bf16[1024,400]{0,1:T(8,128)(2,1)}, bf16[1024,400]{0,1:T(8,128)(2,1)S(1)}, u32[]{:S(2)}) copy-start(bf16[1024,400]{0,1:T(8,128)(2,1)S(1)} %get-tuple-element.339) | copy-start | bytes 2457604 | tf_op jit(solution)/shard_map/while
  71.0 1.1 copy-start
  74.5 2.6 copy-start.1
  111.5 280.5 %reduce-scatter.5.cloned.1.call-start = ((), (), s32[]{:S(2)}) async-start(), calls=%async_computation.3 | async-start | bytes 1843200 | tf_op jit(solution)/shard_map/reduce_scatter | solution.py:115
  111.6 254.6 %copy-start.7 = (f32[16]{0:T(128)S(1)}, f32[16]{0:T(128)}, u32[]{:S(2)}) copy-start(f32[16]{0:T(128)} %param.20) | copy-start | bytes 196
  111.6 256.8 %copy-start.8 = (f32[128,1]{0,1:T(1,128)S(1)}, f32[128,1]{0,1:T(1,128)}, u32[]{:S(2)}) copy-start(f32[128,1]{0,1:T(1,128)} %param.16) | copy-start | bytes 1540
  111.6 257.3 %copy-start.5 = (f32[128,1,400]{0,2,1:T(8,128)S(1)}, f32[128,1,400]{0,2,1:T(8,128)}, u32[]{:S(2)}) copy-start(f32[128,1,400]{0,2,1:T(8,128)} %param.15) | copy-start | bytes 614404
  113.3 279.7 %copy-start.9 = (f32[128,1]{0,1:T(1,128)S(1)}, f32[128,1]{0,1:T(1,128)}, u32[]{:S(2)}) copy-start(f32[128,1]{0,1:T(1,128)} %param.18) | copy-start | bytes 1540
  113.3 280.2 %copy-start.6 = (f32[128,1,400]{0,2,1:T(8,128)S(1)}, f32[128,1,400]{0,2,1:T(8,128)}, u32[]{:S(2)}) copy-start(f32[128,1,400]{0,2,1:T(8,128)} %param.17) | copy-start | bytes 614404
Sparse Core Ops, SparseCore 0:
  111.7 237.8 reduce-scatter.2
  353.0 38.9 reduce-scatter.4
where the time goes:
time: 405 us; the launch traced here: 402 us
  blocking collectives  279 us (69%)
  other arithmetic  40.6 us (10%)
  local copies, waits for them, and re-layouts  35.9 us (9%)
  waiting for transfers between devices  21.5 us (5%)
  between operations  14.8 us (4%)
  matrix products  10.3 us (3%)
    psum x1, blocking collectives, body(): rel_grad = lax.psum(rel_sum, ('src', 'dst'))  253 us
    reduce_scatter x1, waiting for transfers between devices, body(): dst_grad = lax.psum_scatter(dst_sum, 'src', scatter_dimension=0, tiled=True)  21.4 us
    scatter-add x2, other arithmetic, accumulate(): dst_grad = dst_grad.at[dst_idx].add(dst_pos).at[neg_idx].add(dst_neg)  16.1 us
    all_gather x1, blocking collectives, body(): lax.all_gather(src_table.astype(jnp.bfloat16), 'dst', axis=0, tiled=True)  13.5 us
    all_gather x1, blocking collectives, body(): lax.all_gather(dst_table.astype(jnp.bfloat16), 'src', axis=0, tiled=True)  12.5 us
    gather x2, local copies, waits for them, and re-layouts, block_terms(): dst_emb = jnp.take(dst_part, dst_idx, axis=0)  8.69 us
    gather x2, local copies, waits for them, and re-layouts, block_terms(): src_emb = jnp.take(src_part, src_idx, axis=0)  8.38 us
  transfers between devices with their start and end apart: 2, of which 1 were waited for; matrix products, arithmetic and copies ran while one was open for 2% of the time, Pallas kernels for 0%

commit v1 on v0

v1 whole, which is shorter than its diff:
```python
import functools

import jax
import jax.numpy as jnp
from jax import lax
from jax.experimental import pallas as pl
from jax.experimental.pallas import tpu as pltpu
from jax.sharding import PartitionSpec as P

LEARN_RATE = 0.1
CHUNK = 512
LOWEST = -1e30

NN = (((1,), (0,)), ((), ()))
NT = (((1,), (1,)), ((), ()))


def mm(a, b, dims=NN):
    return lax.dot_general(a, b, dims, preferred_element_type=jnp.float32)


def split(x):
    high = x.astype(jnp.bfloat16)
    return high, (x - high.astype(jnp.float32)).astype(jnp.bfloat16)


def one_hot(rows, idx):
    row = lax.broadcasted_iota(jnp.int32, (rows, idx.shape[1]), 0)
    return (row == idx).astype(jnp.float32).astype(jnp.bfloat16)


def bucket_kernel(
    per_block,
    count_ref,
    s_ref,
    t_ref,
    r_ref,
    neg_ref,
    src_t_ref,
    dst_ref,
    dst_t_ref,
    rel_parts_ref,
    src_grad_ref,
    dst_grad_ref,
    rel_grad_ref,
    times_ref,
):
    src_grad_ref[...] = jnp.zeros_like(src_grad_ref)
    dst_grad_ref[...] = jnp.zeros_like(dst_grad_ref)
    rel_grad_ref[...] = jnp.zeros_like(rel_grad_ref)
    count = count_ref[0]
    chunk = s_ref.shape[2]
    src_rows = src_t_ref.shape[1]
    dst_rows = dst_ref.shape[0]
    relations = rel_grad_ref.shape[1]

    @pl.loop(0, (count + chunk - 1) // chunk)
    def _(step):
        @pl.when(lax.rem(step, per_block) == 0)
        def _():
            neg = neg_ref[lax.div(step, per_block)]
            row = lax.broadcasted_iota(jnp.int32, (dst_rows, neg.shape[1]), 0)
            times = jnp.sum((row == neg).astype(jnp.float32), axis=1, keepdims=True)
            times_ref[...] = jnp.broadcast_to(times, times_ref.shape)

        slots = step * chunk + lax.broadcasted_iota(jnp.int32, (1, chunk), 1)
        valid = (slots < count).astype(jnp.float32)
        src_hot = one_hot(src_rows, s_ref[step])
        rel_hot = one_hot(relations, r_ref[step])
        src_emb = mm(src_t_ref[...], src_hot)
        rel_rows = mm(rel_parts_ref[...], jnp.concatenate([rel_hot] * 3, axis=0))
        query = (src_emb * rel_rows).astype(jnp.bfloat16)
        score = mm(dst_ref[...], query)
        is_pos = lax.broadcasted_iota(jnp.int32, score.shape, 0) == t_ref[step]
        times = times_ref[...]
        times = jnp.where(is_pos, times + 1.0, times)
        score = jnp.where(times > 0.0, score, LOWEST)
        top = jnp.max(score, axis=0, keepdims=True)
        terms = times * jnp.exp(score - top)
        weight = terms * (valid / jnp.sum(terms, axis=0, keepdims=True))
        weight = jnp.where(is_pos, weight - valid, weight)
        high, low = split(weight)
        dst_grad_ref[...] += mm(high, query, NT) + mm(low, query, NT)
        dquery = mm(dst_t_ref[...], high) + mm(dst_t_ref[...], low)
        high, low = split(dquery * rel_rows)
        src_grad_ref[...] += mm(src_hot, high, NT) + mm(src_hot, low, NT)
        high, low = split(dquery * src_emb)
        rel_grad_ref[...] += mm(high, rel_hot, NT) + mm(low, rel_hot, NT)


def bucket_grads(src_part, dst_part, rel_table, s_all, t_all, r_all, negs, count):
    blocks, negatives = negs.shape
    width_block = s_all.shape[0] // blocks
    chunk = CHUNK if width_block % CHUNK == 0 else width_block
    steps = s_all.shape[0] // chunk
    high = lax.reduce_precision(rel_table, 8, 7)
    middle = lax.reduce_precision(rel_table - high, 8, 7)
    rel_parts = jnp.concatenate([high, middle, rel_table - high - middle], axis=0)
    vmem = pl.BlockSpec(memory_space=pltpu.VMEM)
    width = rel_table.shape[1]
    src_sum, dst_sum, rel_sum = pl.pallas_call(
        functools.partial(bucket_kernel, width_block // chunk),
        out_shape=(
            jax.ShapeDtypeStruct(src_part.shape, jnp.float32),
            jax.ShapeDtypeStruct(dst_part.shape, jnp.float32),
            jax.ShapeDtypeStruct((width, rel_table.shape[0]), jnp.float32),
        ),
        in_specs=[pl.BlockSpec(memory_space=pltpu.SMEM)] + [vmem] * 8,
        out_specs=[vmem] * 3,
        scratch_shapes=[pltpu.VMEM((dst_part.shape[0], chunk), jnp.float32)],
        compiler_params=pltpu.CompilerParams(vmem_limit_bytes=56 * 2**20),
    )(
        count.reshape(1),
        s_all.reshape(steps, 1, chunk),
        t_all.reshape(steps, 1, chunk),
        r_all.reshape(steps, 1, chunk),
        negs.reshape(blocks, 1, negatives),
        src_part.T,
        dst_part,
        dst_part.T,
        rel_parts.astype(jnp.bfloat16).T,
    )
    return src_sum, dst_sum, rel_sum.T


def adagrad(table, state, grad):
    new_state = state + jnp.mean(grad * grad, axis=-1)
    return (table - LEARN_RATE * grad / jnp.sqrt(new_state)[..., None], new_state)


def body(
    src_table,
    src_state,
    dst_table,
    dst_state,
    rel_table,
    rel_state,
    src_rows,
    dst_rows,
    rel_ids,
    counts,
    neg_rows,
):
    rows, _, width = src_table.shape
    src_part = lax.all_gather(src_table.astype(jnp.bfloat16), "dst", axis=0, tiled=True).reshape(
        -1, width
    )
    dst_part = lax.all_gather(dst_table.astype(jnp.bfloat16), "src", axis=0, tiled=True).reshape(
        -1, width
    )
    s_all = src_rows.reshape(-1)
    t_all = dst_rows.reshape(-1)
    r_all = rel_ids.reshape(-1)
    negs = neg_rows.reshape(neg_rows.shape[2], neg_rows.shape[3])
    count = counts.reshape(())
    src_sum, dst_sum, rel_sum = bucket_grads(
        src_part, dst_part, rel_table, s_all, t_all, r_all, negs, count
    )
    src_grad = lax.psum_scatter(src_sum, "dst", scatter_dimension=0, tiled=True)
    dst_grad = lax.psum_scatter(dst_sum, "src", scatter_dimension=0, tiled=True)
    rel_grad = lax.psum(rel_sum, ("src", "dst"))
    new_src, new_src_state = adagrad(src_table, src_state, src_grad.reshape(src_table.shape))
    new_dst, new_dst_state = adagrad(dst_table, dst_state, dst_grad.reshape(dst_table.shape))
    new_rel, new_rel_state = adagrad(rel_table, rel_state, rel_grad)
    return (new_src, new_src_state, new_dst, new_dst_state, new_rel, new_rel_state)


def solution(mesh):
    return jax.shard_map(
        body,
        mesh=mesh,
        in_specs=(
            P("dst", "src", None),
            P("dst", "src"),
            P("src", "dst", None),
            P("src", "dst"),
            P(),
            P(),
            P("src", "dst", None),
            P("src", "dst", None),
            P("src", "dst", None),
            P("src", "dst"),
            P("src", "dst", None, None),
        ),
        out_specs=(
            P("dst", "src", None),
            P("dst", "src"),
            P("src", "dst", None),
            P("src", "dst"),
            P(),
            P(),
        ),
        check_vma=False,
    )
```

time: 405 us -> 166 us (0.41)
  blocking collectives: 279 us -> 104 us
  other arithmetic: 40.6 us -> 7.62 us
  local copies, waits for them, and re-layouts: 35.9 us -> 5.44 us
  matrix products: 10.3 us -> 0 us
  Pallas kernels: 0 us -> 9.19 us
    psum x1, blocking collectives: 253 us -> 79.2 us  [body(): rel_grad = lax.psum(rel_sum, ('src', 'dst'))]
    scatter-add x3 -> x0, other arithmetic: 23.7 us -> none  [the longest x2 16.1 us: accumulate(): dst_grad = dst_grad.at[dst_idx].add(dst_pos).at[neg_idx].add(dst_neg)]
    gather x5 -> x0, local copies, waits for them, and re-layouts: 23.5 us -> none  [the longest x2 8.69 us: block_terms(): dst_emb = jnp.take(dst_part, dst_idx, axis=0)]
    dot_general x5 -> x0, matrix products: 10.3 us -> none  [the longest x1 2.79 us: block_terms(): rel_rows = jnp.dot(onehot, rel_table, precision=lax.Precision.HIGHEST)]
    pallas_call x0 -> x1, Pallas kernels: none -> 9.19 us  [bucket_grads(): pl.pallas_call(functools.partial(bucket_kernel, width_block // chunk), ou...]
    mul x2 -> x0, local copies, waits for them, and re-layouts: 5.65 us -> none  [the longest x1 2.84 us: block_terms(): src_term = dquery * rel_rows]
    while x12 -> x0, local copies, waits for them, and re-layouts: 5.58 us -> none  [the longest x4 5.22 us: body(): src_sum, dst_sum, rel_sum = lax.fori_loop(0, active, accumulate, start)]
  transfers between devices with their start and end apart: 2 -> 2, of which waited for: 1 -> 1; matrix products, arithmetic and copies ran while one was open for 2% -> 3% of each run, Pallas kernels for 0% -> 0%
where the time goes in v1:
time: 166 us
  blocking collectives  104 us (63%)
  waiting for transfers between devices  24.7 us (15%)
  between operations  14.9 us (9%)
  Pallas kernels  9.19 us (6%)
  other arithmetic  7.62 us (5%)
  local copies, waits for them, and re-layouts  5.44 us (3%)
    psum x1, blocking collectives, body(): rel_grad = lax.psum(rel_sum, ('src', 'dst'))  79.2 us
    reduce_scatter x1, waiting for transfers between devices, body(): dst_grad = lax.psum_scatter(dst_sum, 'src', scatter_dimension=0, tiled=True)  24 us
    all_gather x1, blocking collectives, body(): lax.all_gather(src_table.astype(jnp.bfloat16), 'dst', axis=0, tiled=True)  13 us
    all_gather x1, blocking collectives, body(): lax.all_gather(dst_table.astype(jnp.bfloat16), 'src', axis=0, tiled=True)  12.1 us
    pallas_call x1, Pallas kernels, bucket_grads(): pl.pallas_call(functools.partial(bucket_kernel, width_block // chunk), ou...  9.19 us
  transfers between devices with their start and end apart: 2, of which 1 were waited for; matrix products, arithmetic and copies ran while one was open for 3% of the time, Pallas kernels for 0%

profile of v1, /device:TPU:1, one launch (start us, length us, event | category | flops | bytes accessed | tf_op | source)
XLA Modules:
  0.0 166.1 jit_solution(13634745775194482325)
XLA Ops:
  7.2 0.0 reduce-scatter.3.cloned.1.call-start
  7.2 0.8 reduce-precision_convert_fusion.1
  8.0 0.0 copy-start.5
  8.1 0.8 copy.26
  8.8 0.9 convert_element_type.8
  9.8 12.1 %all_gather.7 = bf16[1024,1,400]{0,2,1:T(8,128)(2,1)S(1)} all-gather(bf16[128,1,400]{0,2,1:T(8,128)(2,1)S(1)} %convert_element_type.8), channel_id=1, replica_groups=mesh['src'=8,'dst'=4] {'src'}, dimensions={0}, use_global_device_ids=true | all-gather | bytes 921600 | tf_op jit(solution)/shard_map/all_gather | solution.py:148
  21.8 1.3 copy.27.dst_ref
  23.1 13.0 %all_gather.6 = bf16[512,1,400]{0,2,1:T(8,128)(2,1)} all-gather(bf16[128,1,400]{0,2,1:T(8,128)(2,1)S(1)} %convert_element_type.7), channel_id=1, replica_groups=mesh['src'=8,'dst'=4] {'dst'}, dimensions={0}, use_global_device_ids=true | all-gather | bytes 512000 | tf_op jit(solution)/shard_map/all_gather | solution.py:145
  36.1 0.6 reshape_reshape.19.neg_ref
  37.4 9.2 %shard_map.154 = (f32[512,400]{1,0:T(8,128)}, f32[1024,400]{1,0:T(8,128)}, f32[400,16]{1,0:T(8,128)}) custom-call(s32[1]{0:T(128)} %bitcast.26.count_ref, s32[8,1,512]{2,1,0:T(1,128)} %bitcast.32, s32[8,1,512]{2,1,0:T(1,128)} %bitcast.33, s32[8,1,512]{2,1,0:T(1,128)} %bitcast.34, s32[4,1,1024]{2,1,0:T(1,128)} %reshape_reshape.19.neg_ref, ...), custom_call_target="tpu_custom_call" | custom-call | tf_op jit(solution)/shard_map/pallas_call | solution.py:101
  46.6 0.0 reduce-scatter.3.cloned.1.call-update
  46.6 0.0 copy-start.6
  46.6 0.0 reduce-scatter.5.cloned.1.call-start
  46.7 0.7 reduce-scatter.5.cloned.1.call-update
  47.4 0.1 copy.30
  47.5 0.0 copy-done.1
  47.5 0.0 copy-start.8
  47.6 0.1 copy.29
  47.7 0.1 copy.28
  47.8 79.2 %psum.7 = f32[16,400]{0,1:T(8,128)S(1)} all-reduce(f32[16,400]{0,1:T(8,128)S(1)} %bitcast.31), channel_id=1, replica_groups=mesh['src'=8,'dst'=4] {'src','dst'}, use_global_device_ids=true, to_apply=%region_4.0 | all-reduce | flops 6400 | bytes 51200 | tf_op jit(solution)/shard_map/psum | solution.py:161
  127.0 0.1 multiply_reduce_fusion.2
  127.1 0.5 fusion.1
  127.6 0.7 copy.33
  128.4 1.1 multiply_reduce_fusion.1
  129.4 0.5 sqrt_bitcast_fusion.1
  129.9 1.0 bitcast_subtract_fusion.1
  131.0 0.8 copy.31
  131.8 24.0 %reduce-scatter.5.cloned.1.call-done = f32[128,400]{1,0:T(8,128)} async-done(((f32[1024,400]{1,0:T(8,128)}), f32[128,400]{1,0:T(8,128)}) %reduce-scatter.5.cloned.1.call-update) | async-done | bytes 204816 | tf_op jit(solution)/shard_map/reduce_scatter | solution.py:160
  155.8 1.1 multiply_reduce_fusion
  156.8 0.5 sqrt_bitcast_fusion
  157.4 1.0 bitcast_subtract_fusion
  158.4 0.8 copy.32
  (18 shorter events, 0.1 us)
Async XLA Ops:
  7.2 15.9 %copy-start.2 = (f32[128,1,400]{0,2,1:T(8,128)S(1)}, f32[128,1,400]{0,2,1:T(8,128)}, u32[]{:S(2)}) copy-start(f32[128,1,400]{0,2,1:T(8,128)} %param.11) | copy-start | bytes 614404
  7.2 121.2 %reduce-scatter.3.cloned.1.call-start = ((), (), s32[]{:S(2)}) async-start(), calls=%async_computation.2 | async-start | bytes 1310720 | tf_op jit(solution)/shard_map/reduce_scatter | solution.py:159
  8.0 28.1 %copy-start.5 = (s32[1,1,4,1024]{3,2,1,0:T(4,128)S(1)}, s32[1,1,4,1024]{3,2,1,0:T(4,128)}, u32[]{:S(2)}) copy-start(s32[1,1,4,1024]{3,2,1,0:T(4,128)} %param.21) | copy-start | bytes 49156
  21.8 15.6 %copy-start = (bf16[1024,1,400]{0,2,1:T(8,128)(2,1)}, bf16[1024,1,400]{0,2,1:T(8,128)(2,1)S(1)}, u32[]{:S(2)}) copy-start(bf16[1024,1,400]{0,2,1:T(8,128)(2,1)S(1)} %all_gather.7) | copy-start | bytes 2457604
  46.6 0.8 copy-start.4
  46.6 0.9 copy-start.1
  46.6 1.2 copy-start.3
  46.6 80.5 %copy-start.6 = (f32[16]{0:T(128)S(1)}, f32[16]{0:T(128)}, u32[]{:S(2)}) copy-start(f32[16]{0:T(128)} %param.16) | copy-start | bytes 196
  46.6 109.1 %reduce-scatter.5.cloned.1.call-start = ((), (), s32[]{:S(2)}) async-start(), calls=%async_computation.3 | async-start | bytes 2359296 | tf_op jit(solution)/shard_map/reduce_scatter | solution.py:160
  46.7 82.7 %copy-start.7 = (f32[128,1]{0,1:T(1,128)S(1)}, f32[128,1]{0,1:T(1,128)}, u32[]{:S(2)}) copy-start(f32[128,1]{0,1:T(1,128)} %param.12) | copy-start | bytes 1540
  47.5 109.3 %copy-start.8 = (f32[128,1]{0,1:T(1,128)S(1)}, f32[128,1]{0,1:T(1,128)}, u32[]{:S(2)}) copy-start(f32[128,1]{0,1:T(1,128)} %param.14) | copy-start | bytes 1540
Sparse Core Ops, SparseCore 0:
  46.8 65.1 reduce-scatter.2
  115.6 40.1 reduce-scatter.4

commit v2 on v1

--- a/solution.py
+++ b/solution.py
@@ -42,6 +42,7 @@
     rel_parts_ref,
     src_grad_ref,
     dst_grad_ref,
+    rel_sum_ref,
     rel_grad_ref,
     times_ref,
 ):
@@ -80,15 +81,193 @@
         weight = terms * (valid / jnp.sum(terms, axis=0, keepdims=True))
         weight = jnp.where(is_pos, weight - valid, weight)
         high, low = split(weight)
-        dst_grad_ref[...] += mm(high, query, NT) + mm(low, query, NT)
+        dst_grad_ref[...] += mm(query, high, NT) + mm(query, low, NT)
         dquery = mm(dst_t_ref[...], high) + mm(dst_t_ref[...], low)
         high, low = split(dquery * rel_rows)
-        src_grad_ref[...] += mm(src_hot, high, NT) + mm(src_hot, low, NT)
+        src_grad_ref[...] += mm(high, src_hot, NT) + mm(low, src_hot, NT)
         high, low = split(dquery * src_emb)
         rel_grad_ref[...] += mm(high, rel_hot, NT) + mm(low, rel_hot, NT)
 
-
-def bucket_grads(src_part, dst_part, rel_table, s_all, t_all, r_all, negs, count):
+    row = lax.broadcasted_iota(jnp.int32, (relations, relations), 0)
+    column = lax.broadcasted_iota(jnp.int32, (relations, relations), 1)
+    rel_sum_ref[...] = lax.dot_general(
+        (row == column).astype(jnp.float32),
+        rel_grad_ref[...],
+        NT,
+        precision=lax.Precision.HIGHEST,
+        preferred_element_type=jnp.float32,
+    )
+
+
+def exchange(axis, n, pairs, send_sem, recv_sem):
+    me = lax.axis_index(axis)
+    copies = []
+    for k in range(1, n):
+        peer = lax.rem(me + k, n)
+        source, target = pairs(me, peer)
+        copies.append(
+            pltpu.make_async_remote_copy(
+                src_ref=source,
+                dst_ref=target,
+                send_sem=send_sem.at[k - 1],
+                recv_sem=recv_sem.at[k - 1],
+                device_id={axis: peer},
+                device_id_type=pl.DeviceIdType.MESH,
+            )
+        )
+    for copy in copies:
+        copy.start()
+    return copies
+
+
+def greet(sizes):
+    barrier = pltpu.get_barrier_semaphore()
+    for axis, n in sizes:
+        me = lax.axis_index(axis)
+        for k in range(1, n):
+            pl.semaphore_signal(
+                barrier,
+                inc=1,
+                device_id={axis: lax.rem(me + k, n)},
+                device_id_type=pl.DeviceIdType.MESH,
+            )
+    pl.semaphore_wait(barrier, sum(n - 1 for _, n in sizes))
+
+
+def lanes(index, rows):
+    return pl.ds(pl.multiple_of(index * rows, rows), rows)
+
+
+def gather_kernel(n_src, n_dst, src_ref, dst_ref, src_all, dst_all, sends, recvs, send2, recv2):
+    greet((("src", n_src), ("dst", n_dst)))
+    rows = dst_ref.shape[1]
+    mine = lanes(lax.axis_index("src"), rows)
+    copies = exchange(
+        "src", n_src, lambda me, peer: (dst_ref, dst_all.at[:, lanes(me, rows)]), sends, recvs
+    )
+    own_rows = src_ref.shape[1]
+    own = lanes(lax.axis_index("dst"), own_rows)
+    copies += exchange(
+        "dst", n_dst, lambda me, peer: (src_ref, src_all.at[:, lanes(me, own_rows)]), send2, recv2
+    )
+    dst_all[:, mine] = dst_ref[...]
+    src_all[:, own] = src_ref[...]
+    for copy in copies:
+        copy.wait()
+
+
+def gather(src_low, dst_low, n_src, n_dst):
+    vmem = pl.BlockSpec(memory_space=pltpu.VMEM)
+    dma = pltpu.SemaphoreType.DMA
+    width = src_low.shape[0]
+    return pl.pallas_call(
+        functools.partial(gather_kernel, n_src, n_dst),
+        out_shape=(
+            jax.ShapeDtypeStruct((width, src_low.shape[1] * n_dst), jnp.bfloat16),
+            jax.ShapeDtypeStruct((width, dst_low.shape[1] * n_src), jnp.bfloat16),
+        ),
+        in_specs=[vmem] * 2,
+        out_specs=[vmem] * 2,
+        scratch_shapes=[
+            dma((n_src - 1,)),
+            dma((n_src - 1,)),
+            dma((n_dst - 1,)),
+            dma((n_dst - 1,)),
+        ],
+        compiler_params=pltpu.CompilerParams(
+            collective_id=0, has_side_effects=True, vmem_limit_bytes=32 * 2**20
+        ),
+    )(src_low, dst_low)
+
+
+def total(slots, n):
+    value = slots[0]
+    for k in range(1, n):
+        value = value + slots[k]
+    return value
+
+
+def reduce_kernel(
+    n_src,
+    n_dst,
+    src_ref,
+    dst_ref,
+    rel_ref,
+    src_out,
+    dst_out,
+    rel_out,
+    src_slots,
+    dst_slots,
+    rel_slots,
+    rel_slots2,
+    part,
+    *sems,
+):
+    greet((("src", n_src), ("dst", n_dst)))
+    i, j = lax.axis_index("src"), lax.axis_index("dst")
+    dst_rows, src_rows = dst_out.shape[1], src_out.shape[1]
+    first = exchange("src", n_src, lambda me, peer: (rel_ref, rel_slots.at[me]), *sems[0:2])
+    copies = exchange(
+        "src",
+        n_src,
+        lambda me, peer: (dst_ref.at[:, lanes(peer, dst_rows)], dst_slots.at[me]),
+        *sems[2:4],
+    )
+    src_copies = exchange(
+        "dst",
+        n_dst,
+        lambda me, peer: (src_ref.at[:, lanes(peer, src_rows)], src_slots.at[me]),
+        *sems[4:6],
+    )
+    rel_slots[i] = rel_ref[...]
+    dst_slots[i] = dst_ref[:, lanes(i, dst_rows)]
+    src_slots[j] = src_ref[:, lanes(j, src_rows)]
+    for copy in first:
+        copy.wait()
+    part[...] = total(rel_slots, n_src)
+    rel_slots2[j] = part[...]
+    second = exchange("dst", n_dst, lambda me, peer: (part, rel_slots2.at[me]), *sems[6:8])
+    for copy in src_copies:
+        copy.wait()
+    src_out[...] = total(src_slots, n_dst)
+    for copy in second:
+        copy.wait()
+    rel_out[...] = total(rel_slots2, n_dst)
+    for copy in copies:
+        copy.wait()
+    dst_out[...] = total(dst_slots, n_src)
+
+
+def reduce(src_sum, dst_sum, rel_sum, n_src, n_dst):
+    vmem = pl.BlockSpec(memory_space=pltpu.VMEM)
+    dma = pltpu.SemaphoreType.DMA
+    width = src_sum.shape[0]
+    src_piece = (width, src_sum.shape[1] // n_dst)
+    dst_piece = (width, dst_sum.shape[1] // n_src)
+    counts = (n_src, n_src, n_dst, n_dst)
+    return pl.pallas_call(
+        functools.partial(reduce_kernel, n_src, n_dst),
+        out_shape=tuple(
+            jax.ShapeDtypeStruct(shape, jnp.float32)
+            for shape in (src_piece, dst_piece, rel_sum.shape)
+        ),
+        in_specs=[vmem] * 3,
+        out_specs=[vmem] * 3,
+        scratch_shapes=[
+            pltpu.VMEM((n_dst,) + src_piece, jnp.float32),
+            pltpu.VMEM((n_src,) + dst_piece, jnp.float32),
+            pltpu.VMEM((n_src,) + rel_sum.shape, jnp.float32),
+            pltpu.VMEM((n_dst,) + rel_sum.shape, jnp.float32),
+            pltpu.VMEM(rel_sum.shape, jnp.float32),
+        ]
+        + [dma((n - 1,)) for n in counts for _ in range(2)],
+        compiler_params=pltpu.CompilerParams(
+            collective_id=1, has_side_effects=True, vmem_limit_bytes=48 * 2**20
+        ),
+    )(src_sum, dst_sum, rel_sum)
+
+
+def bucket_grads(src_t, dst_t, rel_table, s_all, t_all, r_all, negs, count):
     blocks, negatives = negs.shape
     width_block = s_all.shape[0] // blocks
     chunk = CHUNK if width_block % CHUNK == 0 else width_block
@@ -101,13 +280,16 @@
     src_sum, dst_sum, rel_sum = pl.pallas_call(
         functools.partial(bucket_kernel, width_block // chunk),
         out_shape=(
-            jax.ShapeDtypeStruct(src_part.shape, jnp.float32),
-            jax.ShapeDtypeStruct(dst_part.shape, jnp.float32),
-            jax.ShapeDtypeStruct((width, rel_table.shape[0]), jnp.float32),
+            jax.ShapeDtypeStruct(src_t.shape, jnp.float32),
+            jax.ShapeDtypeStruct(dst_t.shape, jnp.float32),
+            jax.ShapeDtypeStruct(rel_table.shape, jnp.float32),
         ),
         in_specs=[pl.BlockSpec(memory_space=pltpu.SMEM)] + [vmem] * 8,
         out_specs=[vmem] * 3,
-        scratch_shapes=[pltpu.VMEM((dst_part.shape[0], chunk), jnp.float32)],
+        scratch_shapes=[
+            pltpu.VMEM((width, rel_table.shape[0]), jnp.float32),
+            pltpu.VMEM((dst_t.shape[1], chunk), jnp.float32),
+        ],
         compiler_params=pltpu.CompilerParams(vmem_limit_bytes=56 * 2**20),
     )(
         count.reshape(1),
@@ -115,12 +297,12 @@
         t_all.reshape(steps, 1, chunk),
         r_all.reshape(steps, 1, chunk),
         negs.reshape(blocks, 1, negatives),
-        src_part.T,
-        dst_part,
-        dst_part.T,
+        src_t,
+        dst_t.T,
+        dst_t,
         rel_parts.astype(jnp.bfloat16).T,
     )
-    return src_sum, dst_sum, rel_sum.T
+    return src_sum, dst_sum, rel_sum
 
 
 def adagrad(table, state, grad):
@@ -129,6 +311,8 @@
 
 
 def body(
+    n_src,
+    n_dst,
     src_table,
     src_state,
     dst_table,
@@ -141,33 +325,27 @@
     counts,
     neg_rows,
 ):
-    rows, _, width = src_table.shape
-    src_part = lax.all_gather(src_table.astype(jnp.bfloat16), "dst", axis=0, tiled=True).reshape(
-        -1, width
-    )
-    dst_part = lax.all_gather(dst_table.astype(jnp.bfloat16), "src", axis=0, tiled=True).reshape(
-        -1, width
-    )
+    src_low = src_table.astype(jnp.bfloat16)[:, 0, :].T
+    dst_low = dst_table.astype(jnp.bfloat16)[:, 0, :].T
+    src_t, dst_t = gather(src_low, dst_low, n_src, n_dst)
     s_all = src_rows.reshape(-1)
     t_all = dst_rows.reshape(-1)
     r_all = rel_ids.reshape(-1)
     negs = neg_rows.reshape(neg_rows.shape[2], neg_rows.shape[3])
     count = counts.reshape(())
     src_sum, dst_sum, rel_sum = bucket_grads(
-        src_part, dst_part, rel_table, s_all, t_all, r_all, negs, count
-    )
-    src_grad = lax.psum_scatter(src_sum, "dst", scatter_dimension=0, tiled=True)
-    dst_grad = lax.psum_scatter(dst_sum, "src", scatter_dimension=0, tiled=True)
-    rel_grad = lax.psum(rel_sum, ("src", "dst"))
-    new_src, new_src_state = adagrad(src_table, src_state, src_grad.reshape(src_table.shape))
-    new_dst, new_dst_state = adagrad(dst_table, dst_state, dst_grad.reshape(dst_table.shape))
+        src_t, dst_t, rel_table, s_all, t_all, r_all, negs, count
+    )
+    src_grad, dst_grad, rel_grad = reduce(src_sum, dst_sum, rel_sum, n_src, n_dst)
+    new_src, new_src_state = adagrad(src_table, src_state, src_grad.T[:, None, :])
+    new_dst, new_dst_state = adagrad(dst_table, dst_state, dst_grad.T[:, None, :])
     new_rel, new_rel_state = adagrad(rel_table, rel_state, rel_grad)
     return (new_src, new_src_state, new_dst, new_dst_state, new_rel, new_rel_state)
 
 
 def solution(mesh):
     return jax.shard_map(
-        body,
+        functools.partial(body, mesh.shape["src"], mesh.shape["dst"]),
         mesh=mesh,
         in_specs=(
             P("dst", "src", None),

time: 166 us -> 96.9 us (0.58)
  blocking collectives: 104 us -> 0 us
  Pallas kernels: 9.19 us -> 82.4 us
  waiting for transfers between devices: 24.7 us -> 0 us
  between operations: 14.9 us -> 1.35 us
  local copies, waits for them, and re-layouts: 5.44 us -> 7.51 us
  other arithmetic: 7.62 us -> 5.74 us
    psum x1 -> x0, blocking collectives: 79.2 us -> none  [body(): rel_grad = lax.psum(rel_sum, ('src', 'dst'))]
    pallas_call x0 -> x2, Pallas kernels: none -> 59.1 us  [the longest x1 43.7 us: reduce(): pl.pallas_call(functools.partial(reduce_kernel, n_src, n_dst), out_shape=...]
    all_gather x2 -> x0, blocking collectives: 25 us -> none  [the longest x1 13 us: body(): lax.all_gather(src_table.astype(jnp.bfloat16), 'dst', axis=0, tiled=True)]
    reduce_scatter x2 -> x0, waiting for transfers between devices: 24 us -> none  [the longest x1 24 us: body(): dst_grad = lax.psum_scatter(dst_sum, 'src', scatter_dimension=0, tiled=True)]
    pallas_call x1, Pallas kernels: 9.19 us -> 23.3 us  [bucket_grads(): pl.pallas_call(functools.partial(bucket_kernel, width_block // chunk), ou...]
    reduce_sum x3, other arithmetic: 2.18 us -> 0.25 us  [adagrad(): new_state = state + jnp.mean(grad * grad, axis=-1)]
    unnamed x24 -> x22, local copies, waits for them, and re-layouts: 2.78 us -> 4.13 us
  transfers between devices with their start and end apart: 2 -> 0, of which waited for: 1 -> 0; matrix products, arithmetic and copies ran while one was open for 3% -> 0% of each run, Pallas kernels for 0% -> 0%
where the time goes in v2:
time: 96.9 us; the launch traced here: 97 us
  Pallas kernels  82.4 us (85%)
  local copies, waits for them, and re-layouts  7.51 us (8%)
  other arithmetic  5.74 us (6%)
  between operations  1.35 us (1%)
    pallas_call x1, Pallas kernels, reduce(): pl.pallas_call(functools.partial(reduce_kernel, n_src, n_dst), out_shape=...  43.7 us
    pallas_call x1, Pallas kernels, bucket_grads(): pl.pallas_call(functools.partial(bucket_kernel, width_block // chunk), ou...  23.3 us
    pallas_call x1, Pallas kernels, gather(): pl.pallas_call(functools.partial(gather_kernel, n_src, n_dst), out_shape=...  15.4 us
    unnamed x22, local copies, waits for them, and re-layouts  4.13 us
    sub x3, other arithmetic, adagrad(): table - LEARN_RATE * grad / jnp.sqrt(new_state)[..., None]  2.11 us

profile of v2, /device:TPU:1, one launch (start us, length us, event | category | flops | bytes accessed | tf_op | source)
XLA Modules:
  0.0 97.0 jit_solution(10919649465950616796)
XLA Ops:
  1.3 1.3 %reshape_reshape.19.neg_ref = s32[4,1,1024]{2,1,0:T(1,128)} reshape(s32[1,1,4,1024]{3,2,1,0:T(4,128)} %param.21) | data formatting | bytes 32768 | tf_op jit(solution)/shard_map/reshape;reshape | solution.py:299
  2.6 0.8 reduce-precision_convert_fusion.1
  3.4 0.8 copy.21
  4.2 1.1 %convert_bitcast_fusion = (bf16[400,128]{1,0:T(8,128)(2,1)S(1)}, bf16[400,128]{1,0:T(8,128)(2,1)S(1)}) fusion(f32[128,1,400]{0,2,1:T(8,128)} %param.13, f32[128,1,400]{0,2,1:T(8,128)} %param.11), kind=kLoop, calls=%fused_computation.4 | loop fusion | flops 102400 | bytes 614400 | tf_op jit(solution)/shard_map/transpose | solution.py:329
  5.2 15.4 %shard_map.154 = (bf16[400,512]{1,0:T(8,128)(2,1)S(1)}, bf16[400,1024]{1,0:T(8,128)(2,1)S(1)}) custom-call(bf16[400,128]{1,0:T(8,128)(2,1)S(1)} %get-tuple-element.32.src_ref, bf16[400,128]{1,0:T(8,128)(2,1)S(1)} %get-tuple-element.31.dst_ref), custom_call_target="tpu_custom_call" | custom-call | tf_op jit(solution)/shard_map/pallas_call | solution.py:163
  20.6 0.0 copy-start.3
  20.7 0.8 copy-done.3
  21.4 0.0 copy-start
  21.4 1.3 %copy.20 = bf16[400,1024]{0,1:T(8,128)(2,1)} copy(bf16[400,1024]{1,0:T(8,128)(2,1)S(1)} %get-tuple-element.15.dst_t_ref) | data formatting | bytes 1638400 | tf_op jit(solution)/shard_map/pallas_call | solution.py:163
  22.7 0.0 copy-done
  22.7 0.0 copy-start.7
  22.7 23.3 %shard_map.155 = (f32[400,512]{1,0:T(8,128)}, f32[400,1024]{1,0:T(8,128)}, f32[16,400]{1,0:T(8,128)}) custom-call(s32[1]{0:T(128)} %bitcast.32.count_ref, s32[8,1,512]{2,1,0:T(1,128)} %bitcast.35, s32[8,1,512]{2,1,0:T(1,128)} %bitcast.36, s32[8,1,512]{2,1,0:T(1,128)} %bitcast.37, s32[4,1,1024]{2,1,0:T(1,128)} %reshape_reshape.19.neg_ref, ...), custom_call_target="tpu_custom_call" | custom-call | tf_op jit(solution)/shard_map/pallas_call | solution.py:280
  46.0 0.0 copy-start.1
  46.0 1.4 %copy-done.1 = f32[400,1024]{1,0:T(8,128)S(1)} copy-done((f32[400,1024]{1,0:T(8,128)S(1)}, f32[400,1024]{1,0:T(8,128)}, u32[]{:S(2)}) %copy-start.1) | copy-done | bytes 1638424
  47.5 1.1 %copy-done.2 = f32[400,512]{1,0:T(8,128)S(1)} copy-done((f32[400,512]{1,0:T(8,128)S(1)}, f32[400,512]{1,0:T(8,128)}, u32[]{:S(2)}) %copy-start.2) | copy-done | bytes 819224
  48.6 0.8 copy-done.4
  49.4 43.7 %shard_map.156 = (f32[400,128]{1,0:T(8,128)S(1)}, f32[400,128]{1,0:T(8,128)S(1)}, f32[16,400]{1,0:T(8,128)S(1)}) custom-call(f32[400,512]{1,0:T(8,128)S(1)} %copy-done.2, f32[400,1024]{1,0:T(8,128)S(1)} %copy-done.1, f32[16,400]{1,0:T(8,128)S(1)} %copy-done.4), custom_call_target="tpu_custom_call" | custom-call | tf_op jit(solution)/shard_map/pallas_call | solution.py:248
  93.1 0.1 multiply_reduce_fusion.1
  93.2 0.1 multiply_reduce_fusion
  93.2 0.1 multiply_reduce_fusion.2
  93.3 0.0 copy-done.8
  93.3 0.5 fusion.1
  93.9 0.0 copy-done.7
  93.9 0.7 divide_subtract_fusion
  94.6 0.0 copy-done.9
  94.6 0.5 sqrt_bitcast_fusion
  95.1 0.0 copy-done.5
  95.1 0.7 bitcast_subtract_fusion
  95.8 0.0 copy-done.10
  95.8 0.5 sqrt_bitcast_fusion.1
  96.3 0.0 copy-done.6
  96.3 0.7 bitcast_subtract_fusion.1
  (8 shorter events, 0.0 us)
Async XLA Ops:
  20.6 0.8 copy-start.3
  21.4 1.3 %copy-start = (bf16[400,1024]{1,0:T(8,128)(2,1)}, bf16[400,1024]{1,0:T(8,128)(2,1)S(1)}, u32[]{:S(2)}) copy-start(bf16[400,1024]{1,0:T(8,128)(2,1)S(1)} %get-tuple-element.15.dst_t_ref) | copy-start | bytes 2457604
  22.7 71.2 %copy-start.7 = (f32[16,400]{1,0:T(8,128)S(1)}, f32[16,400]{1,0:T(8,128)}, u32[]{:S(2)}) copy-start(f32[16,400]{1,0:T(8,128)} %param.15) | copy-start | bytes 76804
  22.7 72.4 %copy-start.5 = (f32[128,1,400]{0,2,1:T(8,128)S(1)}, f32[128,1,400]{0,2,1:T(8,128)}, u32[]{:S(2)}) copy-start(f32[128,1,400]{0,2,1:T(8,128)} %param.13) | copy-start | bytes 614404
  46.0 47.3 %copy-start.8 = (f32[16]{0:T(128)S(1)}, f32[16]{0:T(128)}, u32[]{:S(2)}) copy-start(f32[16]{0:T(128)} %param.16) | copy-start | bytes 196
  46.0 48.6 %copy-start.9 = (f32[128,1]{0,1:T(1,128)S(1)}, f32[128,1]{0,1:T(1,128)}, u32[]{:S(2)}) copy-start(f32[128,1]{0,1:T(1,128)} %param.14) | copy-start | bytes 1540
  46.0 1.5 %copy-start.1 = (f32[400,1024]{1,0:T(8,128)S(1)}, f32[400,1024]{1,0:T(8,128)}, u32[]{:S(2)}) copy-start(f32[400,1024]{1,0:T(8,128)} %get-tuple-element.17.dst_ref) | copy-start | bytes 4915204
  47.5 1.1 %copy-start.2 = (f32[400,512]{1,0:T(8,128)S(1)}, f32[400,512]{1,0:T(8,128)}, u32[]{:S(2)}) copy-start(f32[400,512]{1,0:T(8,128)} %get-tuple-element.16.src_ref) | copy-start | bytes 2457604
  48.6 0.8 copy-start.4
  49.4 46.4 %copy-start.10 = (f32[128,1]{0,1:T(1,128)S(1)}, f32[128,1]{0,1:T(1,128)}, u32[]{:S(2)}) copy-start(f32[128,1]{0,1:T(1,128)} %param.12) | copy-start | bytes 1540
  49.4 46.9 %copy-start.6 = (f32[128,1,400]{0,2,1:T(8,128)S(1)}, f32[128,1,400]{0,2,1:T(8,128)}, u32[]{:S(2)}) copy-start(f32[128,1,400]{0,2,1:T(8,128)} %param.11) | copy-start | bytes 614404

commit v3 on v2

--- a/solution.py
+++ b/solution.py
@@ -40,9 +40,11 @@
     dst_ref,
     dst_t_ref,
     rel_parts_ref,
+    src_sum_ref,
+    dst_sum_ref,
+    rel_sum_ref,
     src_grad_ref,
     dst_grad_ref,
-    rel_sum_ref,
     rel_grad_ref,
     times_ref,
 ):
@@ -59,7 +61,7 @@
     def _(step):
         @pl.when(lax.rem(step, per_block) == 0)
         def _():
-            neg = neg_ref[lax.div(step, per_block)]
+            neg = neg_ref[pl.ds(lax.div(step, per_block), 1), :]
             row = lax.broadcasted_iota(jnp.int32, (dst_rows, neg.shape[1]), 0)
             times = jnp.sum((row == neg).astype(jnp.float32), axis=1, keepdims=True)
             times_ref[...] = jnp.broadcast_to(times, times_ref.shape)
@@ -88,6 +90,8 @@
         high, low = split(dquery * src_emb)
         rel_grad_ref[...] += mm(high, rel_hot, NT) + mm(low, rel_hot, NT)
 
+    src_sum_ref[...] = src_grad_ref[...].astype(jnp.bfloat16)
+    dst_sum_ref[...] = dst_grad_ref[...].astype(jnp.bfloat16)
     row = lax.broadcasted_iota(jnp.int32, (relations, relations), 0)
     column = lax.broadcasted_iota(jnp.int32, (relations, relations), 1)
     rel_sum_ref[...] = lax.dot_general(
@@ -138,7 +142,22 @@
     return pl.ds(pl.multiple_of(index * rows, rows), rows)
 
 
-def gather_kernel(n_src, n_dst, src_ref, dst_ref, src_all, dst_all, sends, recvs, send2, recv2):
+def gather_kernel(
+    n_src,
+    n_dst,
+    src_wide,
+    dst_wide,
+    src_all,
+    dst_all,
+    src_ref,
+    dst_ref,
+    sends,
+    recvs,
+    send2,
+    recv2,
+):
+    src_ref[...] = src_wide[...].astype(jnp.bfloat16)
+    dst_ref[...] = dst_wide[...].astype(jnp.bfloat16)
     greet((("src", n_src), ("dst", n_dst)))
     rows = dst_ref.shape[1]
     mine = lanes(lax.axis_index("src"), rows)
@@ -156,19 +175,21 @@
         copy.wait()
 
 
-def gather(src_low, dst_low, n_src, n_dst):
+def gather(src_part, dst_part, n_src, n_dst):
     vmem = pl.BlockSpec(memory_space=pltpu.VMEM)
     dma = pltpu.SemaphoreType.DMA
-    width = src_low.shape[0]
+    width = src_part.shape[0]
     return pl.pallas_call(
         functools.partial(gather_kernel, n_src, n_dst),
         out_shape=(
-            jax.ShapeDtypeStruct((width, src_low.shape[1] * n_dst), jnp.bfloat16),
-            jax.ShapeDtypeStruct((width, dst_low.shape[1] * n_src), jnp.bfloat16),
+            jax.ShapeDtypeStruct((width, src_part.shape[1] * n_dst), jnp.bfloat16),
+            jax.ShapeDtypeStruct((width, dst_part.shape[1] * n_src), jnp.bfloat16),
         ),
         in_specs=[vmem] * 2,
         out_specs=[vmem] * 2,
         scratch_shapes=[
+            pltpu.VMEM(src_part.shape, jnp.bfloat16),
+            pltpu.VMEM(dst_part.shape, jnp.bfloat16),
             dma((n_src - 1,)),
             dma((n_src - 1,)),
             dma((n_dst - 1,)),
@@ -177,13 +198,13 @@
         compiler_params=pltpu.CompilerParams(
             collective_id=0, has_side_effects=True, vmem_limit_bytes=32 * 2**20
         ),
-    )(src_low, dst_low)
+    )(src_part, dst_part)
 
 
 def total(slots, n):
-    value = slots[0]
+    value = slots[0].astype(jnp.float32)
     for k in range(1, n):
-        value = value + slots[k]
+        value = value + slots[k].astype(jnp.float32)
     return value
 
 
@@ -254,8 +275,8 @@
         in_specs=[vmem] * 3,
         out_specs=[vmem] * 3,
         scratch_shapes=[
-            pltpu.VMEM((n_dst,) + src_piece, jnp.float32),
-            pltpu.VMEM((n_src,) + dst_piece, jnp.float32),
+            pltpu.VMEM((n_dst,) + src_piece, jnp.bfloat16),
+            pltpu.VMEM((n_src,) + dst_piece, jnp.bfloat16),
             pltpu.VMEM((n_src,) + rel_sum.shape, jnp.float32),
             pltpu.VMEM((n_dst,) + rel_sum.shape, jnp.float32),
             pltpu.VMEM(rel_sum.shape, jnp.float32),
@@ -268,7 +289,7 @@
 
 
 def bucket_grads(src_t, dst_t, rel_table, s_all, t_all, r_all, negs, count):
-    blocks, negatives = negs.shape
+    blocks = negs.shape[0]
     width_block = s_all.shape[0] // blocks
     chunk = CHUNK if width_block % CHUNK == 0 else width_block
     steps = s_all.shape[0] // chunk
@@ -280,13 +301,15 @@
     src_sum, dst_sum, rel_sum = pl.pallas_call(
         functools.partial(bucket_kernel, width_block // chunk),
         out_shape=(
-            jax.ShapeDtypeStruct(src_t.shape, jnp.float32),
-            jax.ShapeDtypeStruct(dst_t.shape, jnp.float32),
+            jax.ShapeDtypeStruct(src_t.shape, jnp.bfloat16),
+            jax.ShapeDtypeStruct(dst_t.shape, jnp.bfloat16),
             jax.ShapeDtypeStruct(rel_table.shape, jnp.float32),
         ),
         in_specs=[pl.BlockSpec(memory_space=pltpu.SMEM)] + [vmem] * 8,
         out_specs=[vmem] * 3,
         scratch_shapes=[
+            pltpu.VMEM(src_t.shape, jnp.float32),
+            pltpu.VMEM(dst_t.shape, jnp.float32),
             pltpu.VMEM((width, rel_table.shape[0]), jnp.float32),
             pltpu.VMEM((dst_t.shape[1], chunk), jnp.float32),
         ],
@@ -296,7 +319,7 @@
         s_all.reshape(steps, 1, chunk),
         t_all.reshape(steps, 1, chunk),
         r_all.reshape(steps, 1, chunk),
-        negs.reshape(blocks, 1, negatives),
+        negs,
         src_t,
         dst_t.T,
         dst_t,
@@ -325,9 +348,7 @@
     counts,
     neg_rows,
 ):
-    src_low = src_table.astype(jnp.bfloat16)[:, 0, :].T
-    dst_low = dst_table.astype(jnp.bfloat16)[:, 0, :].T
-    src_t, dst_t = gather(src_low, dst_low, n_src, n_dst)
+    src_t, dst_t = gather(src_table[:, 0, :].T, dst_table[:, 0, :].T, n_src, n_dst)
     s_all = src_rows.reshape(-1)
     t_all = dst_rows.reshape(-1)
     r_all = rel_ids.reshape(-1)

time: 96.9 us -> 86.5 us (0.89)
  Pallas kernels: 82.4 us -> 72.7 us
  other arithmetic: 5.74 us -> 4.09 us
    pallas_call x1, Pallas kernels: 43.7 us -> 34.1 us  [reduce(): pl.pallas_call(functools.partial(reduce_kernel, n_src, n_dst), out_shape=...]
    unnamed x22 -> x24, local copies, waits for them, and re-layouts: 4.13 us -> 5.82 us
    another operation x1 -> x0, local copies, waits for them, and re-layouts: 1.33 us -> none  [bucket_grads(): negs.reshape(blocks, 1, negatives)]
    transpose x1 -> x0, other arithmetic: 1.06 us -> none  [body(): dst_low = dst_table.astype(jnp.bfloat16)[:, 0, :].T]
    sub x3 -> x2, other arithmetic: 2.11 us -> 1.51 us  [adagrad(): table - LEARN_RATE * grad / jnp.sqrt(new_state)[..., None]]
where the time goes in v3:
time: 86.5 us; the launch traced here: 86 us
  Pallas kernels  72.7 us (84%)
  local copies, waits for them, and re-layouts  7.85 us (9%)
  other arithmetic  4.09 us (5%)
  between operations  1.38 us (2%)
    pallas_call x1, Pallas kernels, reduce(): pl.pallas_call(functools.partial(reduce_kernel, n_src, n_dst), out_shape=...  34.1 us
    pallas_call x1, Pallas kernels, bucket_grads(): pl.pallas_call(functools.partial(bucket_kernel, width_block // chunk), ou...  23.2 us
    pallas_call x1, Pallas kernels, gather(): pl.pallas_call(functools.partial(gather_kernel, n_src, n_dst), out_shape=...  15.4 us
    unnamed x24, local copies, waits for them, and re-layouts  5.82 us

profile of v3, /device:TPU:1, one launch (start us, length us, event | category | flops | bytes accessed | tf_op | source)
XLA Modules:
  0.0 86.0 jit_solution(14842860761326702377)
XLA Ops:
  0.6 0.0 copy-start.2
  1.3 0.8 reduce-precision_convert_fusion.1
  2.1 0.8 copy.21
  2.9 0.0 copy-done.2
  2.9 0.0 copy-start.3
  2.9 0.9 %copy-done.3 = f32[128,1,400]{0,2,1:T(8,128)S(1)} copy-done((f32[128,1,400]{0,2,1:T(8,128)S(1)}, f32[128,1,400]{0,2,1:T(8,128)}, u32[]{:S(2)}) %copy-start.3) | copy-done | bytes 204824
  3.8 15.4 %shard_map.154 = (bf16[400,512]{1,0:T(8,128)(2,1)S(1)}, bf16[400,1024]{1,0:T(8,128)(2,1)S(1)}) custom-call(f32[400,128]{1,0:T(8,128)S(1)} %bitcast.33, f32[400,128]{1,0:T(8,128)S(1)} %bitcast.32), custom_call_target="tpu_custom_call" | custom-call | tf_op jit(solution)/shard_map/pallas_call | solution.py:182
  19.2 0.0 copy-start.6
  19.2 0.7 copy-done.6
  20.0 0.0 copy-start
  20.0 1.3 %copy.20 = bf16[400,1024]{0,1:T(8,128)(2,1)} copy(bf16[400,1024]{1,0:T(8,128)(2,1)S(1)} %get-tuple-element.15.dst_t_ref) | data formatting | bytes 1638400 | tf_op jit(solution)/shard_map/pallas_call | solution.py:182
  21.3 0.0 copy-done
  21.3 23.2 %shard_map.155 = (bf16[400,512]{1,0:T(8,128)(2,1)}, bf16[400,1024]{1,0:T(8,128)(2,1)}, f32[16,400]{1,0:T(8,128)}) custom-call(s32[1]{0:T(128)} %bitcast.31.count_ref, s32[8,1,512]{2,1,0:T(1,128)} %bitcast.36, s32[8,1,512]{2,1,0:T(1,128)} %bitcast.37, s32[8,1,512]{2,1,0:T(1,128)} %bitcast.38, s32[4,1024]{1,0:T(4,128)} %bitcast.39, ...), custom_call_target="tpu_custom_call" | custom-call | tf_op jit(solution)/shard_map/pallas_call | solution.py:301
  44.4 0.0 copy-start.1
  44.4 1.1 %copy-done.1 = bf16[400,1024]{1,0:T(8,128)(2,1)S(1)} copy-done((bf16[400,1024]{1,0:T(8,128)(2,1)S(1)}, bf16[400,1024]{1,0:T(8,128)(2,1)}, u32[]{:S(2)}) %copy-start.1) | copy-done | bytes 819224
  45.6 1.0 %copy-done.5 = bf16[400,512]{1,0:T(8,128)(2,1)S(1)} copy-done((bf16[400,512]{1,0:T(8,128)(2,1)S(1)}, bf16[400,512]{1,0:T(8,128)(2,1)}, u32[]{:S(2)}) %copy-start.5) | copy-done | bytes 409624
  46.6 0.8 copy-done.7
  47.3 34.1 %shard_map.156 = (f32[400,128]{1,0:T(8,128)S(1)}, f32[400,128]{1,0:T(8,128)S(1)}, f32[16,400]{1,0:T(8,128)S(1)}) custom-call(bf16[400,512]{1,0:T(8,128)(2,1)S(1)} %copy-done.5, bf16[400,1024]{1,0:T(8,128)(2,1)S(1)} %copy-done.1, f32[16,400]{1,0:T(8,128)S(1)} %copy-done.7), custom_call_target="tpu_custom_call" | custom-call | tf_op jit(solution)/shard_map/pallas_call | solution.py:269
  81.5 0.1 multiply_reduce_fusion.1
  81.5 0.1 multiply_reduce_fusion
  81.6 0.0 copy-start.8
  81.6 0.1 multiply_reduce_fusion.2
  81.7 0.6 copy-done.9
  82.3 0.5 fusion.1
  82.8 0.0 copy-done.8
  82.8 0.7 divide_subtract_fusion
  83.5 0.0 copy-done.10
  83.5 0.5 sqrt_bitcast_fusion
  84.0 0.7 copy-done.11
  84.7 0.5 sqrt_bitcast_fusion.1
  85.2 0.0 copy-done.4
  85.2 0.8 bitcast_subtract_fusion
  (7 shorter events, 0.0 us)
Async XLA Ops:
  0.6 2.2 %copy-start.2 = (f32[128,1,400]{0,2,1:T(8,128)S(1)}, f32[128,1,400]{0,2,1:T(8,128)}, u32[]{:S(2)}) copy-start(f32[128,1,400]{0,2,1:T(8,128)} %param.13) | copy-start | bytes 614404
  2.9 0.9 %copy-start.3 = (f32[128,1,400]{0,2,1:T(8,128)S(1)}, f32[128,1,400]{0,2,1:T(8,128)}, u32[]{:S(2)}) copy-start(f32[128,1,400]{0,2,1:T(8,128)} %param.11) | copy-start | bytes 614404
  19.2 0.8 copy-start.6
  20.0 1.3 %copy-start = (bf16[400,1024]{1,0:T(8,128)(2,1)}, bf16[400,1024]{1,0:T(8,128)(2,1)S(1)}, u32[]{:S(2)}) copy-start(bf16[400,1024]{1,0:T(8,128)(2,1)S(1)} %get-tuple-element.15.dst_t_ref) | copy-start | bytes 2457604
  44.4 1.1 %copy-start.1 = (bf16[400,1024]{1,0:T(8,128)(2,1)S(1)}, bf16[400,1024]{1,0:T(8,128)(2,1)}, u32[]{:S(2)}) copy-start(bf16[400,1024]{1,0:T(8,128)(2,1)} %get-tuple-element.17.dst_ref) | copy-start | bytes 2457604
  45.6 1.0 %copy-start.5 = (bf16[400,512]{1,0:T(8,128)(2,1)S(1)}, bf16[400,512]{1,0:T(8,128)(2,1)}, u32[]{:S(2)}) copy-start(bf16[400,512]{1,0:T(8,128)(2,1)} %get-tuple-element.16.src_ref) | copy-start | bytes 1228804
  46.6 0.8 copy-start.7
  81.5 3.7 %copy-start.4 = (f32[128,1,400]{0,2,1:T(8,128)S(1)}, f32[128,1,400]{0,2,1:T(8,128)}, u32[]{:S(2)}) copy-start(f32[128,1,400]{0,2,1:T(8,128)} %param.11) | copy-start | bytes 614404
  81.6 0.7 copy-start.9
  81.6 1.2 %copy-start.8 = (f32[16,400]{1,0:T(8,128)S(1)}, f32[16,400]{1,0:T(8,128)}, u32[]{:S(2)}) copy-start(f32[16,400]{1,0:T(8,128)} %param.15) | copy-start | bytes 76804
  82.8 0.7 copy-start.10
  84.0 0.7 copy-start.11

commit v4 on v3

--- a/solution.py
+++ b/solution.py
@@ -8,7 +8,7 @@
 from jax.sharding import PartitionSpec as P
 
 LEARN_RATE = 0.1
-CHUNK = 512
+CHUNK_ROWS = 2**20
 LOWEST = -1e30
 
 NN = (((1,), (0,)), ((), ()))
@@ -291,7 +291,8 @@
 def bucket_grads(src_t, dst_t, rel_table, s_all, t_all, r_all, negs, count):
     blocks = negs.shape[0]
     width_block = s_all.shape[0] // blocks
-    chunk = CHUNK if width_block % CHUNK == 0 else width_block
+    chunk = min(width_block, max(128, CHUNK_ROWS // dst_t.shape[1]))
+    chunk = chunk if width_block % chunk == 0 else width_block
     steps = s_all.shape[0] // chunk
     high = lax.reduce_precision(rel_table, 8, 7)
     middle = lax.reduce_precision(rel_table - high, 8, 7)

time: 86.5 us -> 83.8 us (0.969)
  Pallas kernels: 72.7 us -> 69.7 us
    pallas_call x1, Pallas kernels: 23.2 us -> 12.3 us  [bucket_grads(): pl.pallas_call(functools.partial(bucket_kernel, width_block // chunk), ou...]
    pallas_call x1, Pallas kernels: 34.1 us -> 42.1 us  [reduce(): pl.pallas_call(functools.partial(reduce_kernel, n_src, n_dst), out_shape=...]
where the time goes in v4:
time: 83.8 us; the launch traced here: 83 us
  Pallas kernels  69.7 us (83%)
  local copies, waits for them, and re-layouts  7.85 us (9%)
  other arithmetic  4.09 us (5%)
  between operations  1.38 us (2%)
    pallas_call x1, Pallas kernels, reduce(): pl.pallas_call(functools.partial(reduce_kernel, n_src, n_dst), out_shape=...  42.1 us
    pallas_call x1, Pallas kernels, gather(): pl.pallas_call(functools.partial(gather_kernel, n_src, n_dst), out_shape=...  15.4 us
    pallas_call x1, Pallas kernels, bucket_grads(): pl.pallas_call(functools.partial(bucket_kernel, width_block // chunk), ou...  12.3 us
    unnamed x24, local copies, waits for them, and re-layouts  5.82 us

profile of v4, /device:TPU:1, one launch (start us, length us, event | category | flops | bytes accessed | tf_op | source)
XLA Modules:
  0.0 83.0 jit_solution(16427451428621165490)
XLA Ops:
  0.6 0.0 copy-start.2
  1.3 0.8 reduce-precision_convert_fusion.1
  2.1 0.8 copy.21
  2.9 0.0 copy-done.2
  2.9 0.9 %copy-done.3 = f32[128,1,400]{0,2,1:T(8,128)S(1)} copy-done((f32[128,1,400]{0,2,1:T(8,128)S(1)}, f32[128,1,400]{0,2,1:T(8,128)}, u32[]{:S(2)}) %copy-start.3) | copy-done | bytes 204824
  3.8 15.4 %shard_map.154 = (bf16[400,512]{1,0:T(8,128)(2,1)S(1)}, bf16[400,1024]{1,0:T(8,128)(2,1)S(1)}) custom-call(f32[400,128]{1,0:T(8,128)S(1)} %bitcast.33, f32[400,128]{1,0:T(8,128)S(1)} %bitcast.32), custom_call_target="tpu_custom_call" | custom-call | tf_op jit(solution)/shard_map/pallas_call | solution.py:182
  19.2 0.0 copy-start.6
  19.2 0.7 copy-done.6
  20.0 0.0 copy-start
  20.0 1.3 %copy.20 = bf16[400,1024]{0,1:T(8,128)(2,1)} copy(bf16[400,1024]{1,0:T(8,128)(2,1)S(1)} %get-tuple-element.15.dst_t_ref) | data formatting | bytes 1638400 | tf_op jit(solution)/shard_map/pallas_call | solution.py:182
  21.3 0.0 copy-done
  21.3 12.3 %shard_map.155 = (bf16[400,512]{1,0:T(8,128)(2,1)}, bf16[400,1024]{1,0:T(8,128)(2,1)}, f32[16,400]{1,0:T(8,128)}) custom-call(s32[1]{0:T(128)} %bitcast.31.count_ref, s32[4,1,1024]{2,1,0:T(1,128)} %bitcast.36, s32[4,1,1024]{2,1,0:T(1,128)} %bitcast.37, s32[4,1,1024]{2,1,0:T(1,128)} %bitcast.38, s32[4,1024]{1,0:T(4,128)} %bitcast.39, ...), custom_call_target="tpu_custom_call" | custom-call | tf_op jit(solution)/shard_map/pallas_call | solution.py:302
  33.5 0.0 copy-start.1
  33.5 1.1 %copy-done.1 = bf16[400,1024]{1,0:T(8,128)(2,1)S(1)} copy-done((bf16[400,1024]{1,0:T(8,128)(2,1)S(1)}, bf16[400,1024]{1,0:T(8,128)(2,1)}, u32[]{:S(2)}) %copy-start.1) | copy-done | bytes 819224
  34.7 0.0 copy-start.5
  34.7 1.0 %copy-done.5 = bf16[400,512]{1,0:T(8,128)(2,1)S(1)} copy-done((bf16[400,512]{1,0:T(8,128)(2,1)S(1)}, bf16[400,512]{1,0:T(8,128)(2,1)}, u32[]{:S(2)}) %copy-start.5) | copy-done | bytes 409624
  35.7 0.8 copy-done.7
  36.4 42.1 %shard_map.156 = (f32[400,128]{1,0:T(8,128)S(1)}, f32[400,128]{1,0:T(8,128)S(1)}, f32[16,400]{1,0:T(8,128)S(1)}) custom-call(bf16[400,512]{1,0:T(8,128)(2,1)S(1)} %copy-done.5, bf16[400,1024]{1,0:T(8,128)(2,1)S(1)} %copy-done.1, f32[16,400]{1,0:T(8,128)S(1)} %copy-done.7), custom_call_target="tpu_custom_call" | custom-call | tf_op jit(solution)/shard_map/pallas_call | solution.py:269
  78.5 0.1 multiply_reduce_fusion.1
  78.6 0.1 multiply_reduce_fusion
  78.6 0.0 copy-start.8
  78.7 0.1 multiply_reduce_fusion.2
  78.8 0.6 copy-done.9
  79.3 0.5 fusion.1
  79.8 0.0 copy-done.8
  79.8 0.7 divide_subtract_fusion
  80.5 0.0 copy-done.10
  80.5 0.5 sqrt_bitcast_fusion
  81.1 0.7 copy-done.11
  81.7 0.5 sqrt_bitcast_fusion.1
  82.2 0.0 copy-done.4
  82.2 0.8 bitcast_subtract_fusion
  (7 shorter events, 0.0 us)
Async XLA Ops:
  0.6 2.2 %copy-start.2 = (f32[128,1,400]{0,2,1:T(8,128)S(1)}, f32[128,1,400]{0,2,1:T(8,128)}, u32[]{:S(2)}) copy-start(f32[128,1,400]{0,2,1:T(8,128)} %param.13) | copy-start | bytes 614404
  2.9 0.9 %copy-start.3 = (f32[128,1,400]{0,2,1:T(8,128)S(1)}, f32[128,1,400]{0,2,1:T(8,128)}, u32[]{:S(2)}) copy-start(f32[128,1,400]{0,2,1:T(8,128)} %param.11) | copy-start | bytes 614404
  19.2 0.8 copy-start.6
  20.0 1.3 %copy-start = (bf16[400,1024]{1,0:T(8,128)(2,1)}, bf16[400,1024]{1,0:T(8,128)(2,1)S(1)}, u32[]{:S(2)}) copy-start(bf16[400,1024]{1,0:T(8,128)(2,1)S(1)} %get-tuple-element.15.dst_t_ref) | copy-start | bytes 2457604
  33.5 1.1 %copy-start.1 = (bf16[400,1024]{1,0:T(8,128)(2,1)S(1)}, bf16[400,1024]{1,0:T(8,128)(2,1)}, u32[]{:S(2)}) copy-start(bf16[400,1024]{1,0:T(8,128)(2,1)} %get-tuple-element.17.dst_ref) | copy-start | bytes 2457604
  34.7 1.0 %copy-start.5 = (bf16[400,512]{1,0:T(8,128)(2,1)S(1)}, bf16[400,512]{1,0:T(8,128)(2,1)}, u32[]{:S(2)}) copy-start(bf16[400,512]{1,0:T(8,128)(2,1)} %get-tuple-element.16.src_ref) | copy-start | bytes 1228804
  35.7 0.8 copy-start.7
  78.6 3.7 %copy-start.4 = (f32[128,1,400]{0,2,1:T(8,128)S(1)}, f32[128,1,400]{0,2,1:T(8,128)}, u32[]{:S(2)}) copy-start(f32[128,1,400]{0,2,1:T(8,128)} %param.11) | copy-start | bytes 614404
  78.6 0.7 copy-start.9
  78.6 1.2 %copy-start.8 = (f32[16,400]{1,0:T(8,128)S(1)}, f32[16,400]{1,0:T(8,128)}, u32[]{:S(2)}) copy-start(f32[16,400]{1,0:T(8,128)} %param.15) | copy-start | bytes 76804
  79.8 0.7 copy-start.10
  81.1 0.7 copy-start.11
